TPU v7x, 32 devices: a whole 2x2x4 slice. The times are simulated.
32 devices in a mesh: state: 2 (over x), wide: 16 (over z, y, core).
Axes of the slice: x: 2, y: 2, z: 4, core: 2. Of those that a mesh axis runs over, the one named last changes fastest.
Arguments:
- block_answers: float32 [32768, 512], P(('state', 'wide')), parts along dimension 0, may hold values from -24 to 24
- block_owner: int32 [32768, 1], P(('state', 'wide')), parts along dimension 0, may hold values from 0 to 15; in each aligned block of 1024 rows (0 to 1023, 1024 to 2047, ...) at most 80 rows name the same one
- block_place: int32 [32768], P(('state', 'wide')), parts along dimension 0, may hold values from 0 to 63
- tract_answers: float32 [2048, 512], P(('state', 'wide')), parts along dimension 0, may hold values from -24 to 24
- tract_county: int32 [2048], P(('state', 'wide')), parts along dimension 0, may hold values from 0 to 87
- county_answers: float32 [176, 512], P('state'), parts along dimension 0, may hold values from -24 to 24
- state_answers: float32 [2, 512], P('state'), parts along dimension 0, may hold values from -24 to 24
- query_members: int32 [2016, 8], replicated, may hold values from 0 to 511, all different within a row
- query_precision: float32 [4, 512], replicated, may hold values from 0.25 to 4
Outputs:
- block_histogram: float32 [32768, 2016], P(('state', 'wide')), parts along dimension 0
- tract_histogram: float32 [2048, 2016], P(('state', 'wide')), parts along dimension 0
- county_histogram: float32 [176, 2016], P('state'), parts along dimension 0
There are 2 independent parts, one for each index of `state`. A program takes and returns all parts, laid end to end along the dimension named above; an argument that names none is the same for every part. Nothing has to cross between parts.
Inputs may be any that keep to these rules, and one draw needn't show every extreme that they name: `block_owner`: in each aligned block of 1024 rows (the blocks of one device) no owner is named by more than 80 rows. `query_members`: each row names 8 different queries, and every query is named by some row.
All inputs are finite; a program needn't handle non-finite values.
Results may differ from a plain program's by a relative error of at most 0.00005.
Values sent between devices are 32-bit elements; how exact they have to be, the bound alone decides.
A program may use at most 128 MiB of HBM per device.

v0:
```python
import functools
import itertools

import jax
import jax.numpy as jnp
from jax import lax
from jax.experimental import pallas as pl
from jax.experimental.pallas import tpu as pltpu
from jax.sharding import PartitionSpec as P

LANES = 128
CHUNKS = 16
MESH = pl.DeviceIdType.MESH
F32 = jnp.float32
BF16 = jnp.bfloat16


def halves(x):
    high = x.astype(BF16)
    return high, (x - high.astype(F32)).astype(BF16)


def product(left, right):
    return jnp.dot(left, right, preferred_element_type=F32)


def two_products(high, low, right):
    return product(high, right) + product(low, right)


def picked(table, row_of):
    groups = table.shape[0]
    count = row_of.shape[0]
    wide = jnp.zeros((count, LANES), F32)
    for g in range(groups):
        wide = jnp.where(row_of // LANES == g, table[g : g + 1, :], wide)
    lane = lax.broadcasted_iota(jnp.int32, (count, LANES), 1)
    return jnp.sum(jnp.where(lane == row_of % LANES, wide, 0.0), axis=1, keepdims=True)


def tree_kernel(
    n,
    ba_ref,
    tof_row_ref,
    tof_col_ref,
    ta_ref,
    tc_ref,
    cs_ref,
    mt_ref,
    qp_ref,
    g1h_ref,
    g1l_ref,
    gsh_ref,
    gsl_ref,
    cover_ref,
    var_ref,
    tab_ref,
    rate_ref,
    hist_ref,
    acc,
    g1,
    gs,
    g2,
    misc,
    misc_send,
    misc_recv,
    send_sems,
    recv_sems,
    *rbufs,
):
    nb = n.bit_length() - 1
    me = lax.axis_index("wide")
    rows, queries = ta_ref.shape
    blocks = ba_ref.shape[0]
    cells = cover_ref.shape[1]
    groups = n * rows // LANES
    counties = rate_ref.shape[0]
    half = queries // 2
    bit = [(me // (1 << b)) % 2 for b in range(nb)]
    orders = [list(range(nb)), [0] + list(range(2, nb)) + [1]]
    cols = [pl.ds(0, half), pl.ds(half, half)]
    used = [0]
    sends = []

    def partner(b):
        return me + (1 - 2 * bit[b]) * (1 << b)

    def remote(src, dst, b):
        k = used[0]
        used[0] += 1
        copy = pltpu.make_async_remote_copy(
            src_ref=src,
            dst_ref=dst,
            send_sem=send_sems.at[k],
            recv_sem=recv_sems.at[k],
            device_id={"wide": partner(b)},
            device_id_type=MESH,
        )
        copy.start()
        sends.append(copy)
        return copy

    def at(values, low=0):
        return tuple(values[b] for b in range(nb - 1, low - 1, -1))

    def scatter_start(g, k):
        order = orders[g]
        values = [slice(None)] * nb
        for b in order[:k]:
            values[b] = bit[b]
        values[order[k]] = 1 - bit[order[k]]
        src = acc.at[at(values) + (slice(None), cols[g])]
        return remote(src, rbufs[g * nb + k], order[k])

    def scatter_add(g, k):
        order = orders[g]
        rest = sorted(order[k + 1 :], reverse=True)
        for combo in itertools.product((0, 1), repeat=len(rest)):
            values = list(bit)
            for b, v in zip(rest, combo):
                values[b] = v
            spot = at(values) + (slice(None), cols[g])
            acc[spot] = acc[spot] + rbufs[g * nb + k][combo + (slice(None), slice(None))]

    def gather_start(buf, order, k, tail, low=0):
        values = list(bit)
        for b in order[:k]:
            values[b] = slice(None)
        ref = buf.at[at(values, low) + tail]
        return remote(ref, ref, order[k])

    barrier = pltpu.get_barrier_semaphore()
    for k in range(1, n):
        pl.semaphore_signal(
            barrier, inc=1, device_id={"wide": lax.rem(me + k, n)}, device_id_type=MESH
        )
    pl.semaphore_wait(barrier, n - 1)

    back = [list(reversed(o)) for o in orders]
    g1[at(bit)] = ta_ref[...] * qp_ref[1:2, :]
    tract_copies = [gather_start(g1, back[g], 0, (slice(None), cols[g])) for g in range(2)]

    tof_row = tof_row_ref[...]
    tof_col = tof_col_ref[...]
    row_hot = (lax.broadcasted_iota(jnp.int32, (groups, blocks), 0) == tof_row // LANES).astype(BF16)
    col_hot = (lax.broadcasted_iota(jnp.int32, (blocks, LANES), 1) == tof_col % LANES).astype(BF16)
    misc[me, :groups, :] = product(row_hot, col_hot)
    lane = lax.broadcasted_iota(jnp.int32, (8, LANES), 1)
    mine = lane // rows == me % (LANES // rows)
    misc[me, groups:, :] = jnp.where(mine, tc_ref[...], 0.0)
    misc_copies = []
    for k in range(1, n):
        copy = pltpu.make_async_remote_copy(
            src_ref=misc.at[me],
            dst_ref=misc.at[me],
            send_sem=misc_send.at[k],
            recv_sem=misc_recv.at[k],
            device_id={"wide": lax.rem(me + k, n)},
            device_id_type=MESH,
        )
        copy.start()
        misc_copies.append(copy)

    xh, xl = halves(ba_ref[...] * qp_ref[0:1, :])
    step = min(4, n)
    for c in range(n // step):
        label = lax.broadcasted_iota(jnp.int32, (step * rows, blocks), 0) + c * step * rows
        hot = (label == tof_row).astype(BF16)
        part = product(hot, xh) + product(hot, xl)
        for s in range(step):
            w = c * step + s
            spot = tuple((w >> b) & 1 for b in range(nb - 1, -1, -1))
            acc[spot] = part[s * rows : (s + 1) * rows]

    sums = [scatter_start(g, 0) for g in range(2)]

    def cover_rows(i, carry):
        start = pl.multiple_of(i * 16, 16)
        label = lax.broadcasted_iota(jnp.int32, (16, cells), 0) + start
        total = jnp.zeros((16, cells), F32)
        for m in range(mt_ref.shape[0]):
            total = total + jnp.where(label == mt_ref[m : m + 1, :], 1.0, 0.0)
        cover_ref[pl.ds(start, 16), :] = total.astype(BF16)
        return carry

    lax.fori_loop(0, queries // 16, cover_rows, 0)
    weights = jnp.concatenate([qp_ref[...], qp_ref[...]], axis=0)
    w0, rest = halves(weights)
    w1, w2 = halves(weights - w0.astype(F32))
    cover = cover_ref[...]
    coverage = product(w0, cover) + product(w1, cover) + product(w2, cover)
    var_ref[...] = 1.0 / coverage

    for k in range(nb):
        for g in range(2):
            sums[g].wait_recv()
            scatter_add(g, k)
            if k + 1 < nb:
                sums[g] = scatter_start(g, k + 1)
        for g in range(2):
            tract_copies[g].wait_recv()
            if k + 1 < nb:
                tract_copies[g] = gather_start(g1, back[g], k + 1, (slice(None), cols[g]))
    gs[at(bit)] = acc[at(bit)]
    sums = [gather_start(gs, back[g], 0, (slice(None), cols[g])) for g in range(2)]

    for copy in misc_copies:
        copy.wait_recv()
    counts = misc[0, :groups, :]
    for d in range(1, n):
        counts = counts + misc[d, :groups, :]
    per = LANES // rows
    county_rows = []
    for j in range(groups):
        row = misc[j * per, groups : groups + 1, :]
        for i in range(1, per):
            row = row + misc[j * per + i, groups : groups + 1, :]
        county_rows.append(row)
    tab_ref[0] = counts
    for j in range(groups):
        tab_ref[1, j : j + 1, :] = county_rows[j]

    def split_into(buf, high_ref, low_ref):
        for w in range(n):
            spot = tuple((w >> b) & 1 for b in range(nb - 1, -1, -1))
            high, low = halves(buf[spot])
            high_ref[w * rows : (w + 1) * rows, :] = high
            low_ref[w * rows : (w + 1) * rows, :] = low

    low_bit = nb - (CHUNKS.bit_length() - 1)
    chunk = me // (1 << low_bit)
    lanes = pl.ds(pl.multiple_of(chunk * LANES, LANES), LANES)
    cov = cover_ref[:, lanes]
    var = var_ref[:, lanes]
    v0, v1, v2, v3 = var[0:1], var[1:2], var[2:3], var[3:4]
    split_into(g1, g1h_ref, g1l_ref)
    tract_part = two_products(g1h_ref[...], g1l_ref[...], cov)
    ch, cl = halves(cs_ref[...])
    upper = two_products(ch, cl, cov)
    county_measured = upper[:counties] * v2
    state_measured = upper[counties : counties + 1] * v3
    n_col = picked(counts, lax.broadcasted_iota(jnp.int32, (n * rows, 1), 0))

    for k in range(nb):
        for g in range(2):
            sums[g].wait_recv()
            if k + 1 < nb:
                sums[g] = gather_start(gs, back[g], k + 1, (slice(None), cols[g]))
    split_into(gs, gsh_ref, gsl_ref)
    sum_part = two_products(gsh_ref[...], gsl_ref[...], cov)
    child_spread = n_col * v0
    scale = 1.0 / (child_spread + v1)
    joined = (n_col * tract_part + sum_part) * (v0 * v1) * scale
    spread = child_spread * v1 * scale
    jh, jl = halves(joined)
    sh, sl = halves(spread)
    county_child = jnp.zeros((counties, LANES), F32)
    county_child_spread = jnp.zeros((counties, LANES), F32)
    for j in range(groups):
        label = lax.broadcasted_iota(jnp.int32, (counties, LANES), 0).astype(F32)
        hot = (label == county_rows[j]).astype(BF16)
        piece = slice(j * LANES, (j + 1) * LANES)
        county_child += product(hot, jh[piece]) + product(hot, jl[piece])
        county_child_spread += product(hot, sh[piece]) + product(hot, sl[piece])
    county_total = county_child_spread + v2
    county_joined = (county_child_spread * county_measured + v2 * county_child) / county_total
    county_spread = county_child_spread * v2 / county_total
    state_sum = jnp.sum(county_joined, axis=0, keepdims=True)
    state_spread = jnp.sum(county_spread, axis=0, keepdims=True)
    state_rate = (state_measured - state_sum) / (state_spread + v3)
    spot = at(bit, low_bit)
    g2[spot + (0,)] = (county_measured - county_child + v2 * state_rate) / county_total
    g2[spot + (1,)] = county_joined + county_spread * state_rate
    short = [[b for b in o if b >= low_bit] for o in back]
    last = [gather_start(g2, short[g], 0, (g,), low_bit) for g in range(2)]
    for k in range(len(short[0])):
        for g in range(2):
            last[g].wait_recv()
            if k + 1 < len(short[0]):
                last[g] = gather_start(g2, short[g], k + 1, (g,), low_bit)
    for c in range(CHUNKS):
        spot = tuple((c >> b) & 1 for b in range(CHUNKS.bit_length() - 2, -1, -1))
        rate_ref[:, c * LANES : (c + 1) * LANES] = g2[spot + (0,)]
        hist_ref[:, c * LANES : (c + 1) * LANES] = g2[spot + (1,)]
    for copy in sends + misc_copies:
        copy.wait_send()


def histogram_kernel(
    ba_ref,
    tof_ref,
    own_ref,
    qp_ref,
    g1h_ref,
    g1l_ref,
    gsh_ref,
    gsl_ref,
    cover_ref,
    var_ref,
    tab_ref,
    rate_ref,
    hist_ref,
    block_ref,
    tract_ref,
    county_ref,
):
    cells = block_ref.shape[1]
    tracts = g1h_ref.shape[0]
    counties = rate_ref.shape[0]
    width = 512

    def gathered(ids):
        count = ids.shape[0]
        hot = (lax.broadcasted_iota(jnp.int32, (count, tracts), 1) == ids).astype(BF16)
        parts = [product(hot, ref[...]).astype(BF16) for ref in (g1h_ref, g1l_ref, gsh_ref, gsl_ref)]
        n_col = picked(tab_ref[0], ids)
        county = picked(tab_ref[1], ids)
        label = lax.broadcasted_iota(jnp.int32, (count, counties), 1).astype(F32)
        return parts, n_col, (label == county).astype(BF16)

    def pieces(start, stop, parts, county_hot):
        cov = cover_ref[:, start:stop]
        rh, rl = halves(rate_ref[:, start:stop])
        above = product(county_hot, rh) + product(county_hot, rl)
        return (
            cov,
            var_ref[0:1, start:stop],
            var_ref[1:2, start:stop],
            two_products(parts[0], parts[1], cov),
            two_products(parts[2], parts[3], cov),
            above,
        )

    parts, n_col, county_hot = gathered(tof_ref[...])
    xh, xl = halves(ba_ref[...] * qp_ref[0:1, :])
    for start in range(0, cells, width):
        stop = min(cells, start + width)
        cov, v0, v1, tract_part, sum_part, above = pieces(start, stop, parts, county_hot)
        rate = (v1 * (tract_part + above) - v0 * sum_part) / (n_col * v0 + v1)
        block_ref[:, start:stop] = v0 * (two_products(xh, xl, cov) + rate)

    @pl.when(pl.program_id(0) == 0)
    def _():
        parts, n_col, county_hot = gathered(own_ref[...])
        for start in range(0, cells, width):
            stop = min(cells, start + width)
            cov, v0, v1, tract_part, sum_part, above = pieces(start, stop, parts, county_hot)
            top = n_col * tract_part + sum_part + n_col * above
            tract_ref[:, start:stop] = v0 * v1 * top / (n_col * v0 + v1)
        county_ref[...] = hist_ref[:, :cells]


def local(
    block_answers,
    block_owner,
    block_place,
    tract_answers,
    tract_county,
    county_answers,
    state_answers,
    query_members,
    query_precision,
):
    n = lax.axis_size("wide")
    nb = n.bit_length() - 1
    blocks, queries = block_answers.shape
    rows = tract_answers.shape[0]
    tracts = rows * n
    cells = query_members.shape[0]
    counties = county_answers.shape[0]
    padded = CHUNKS * LANES
    groups = tracts // LANES
    half = queries // 2
    tof_col = block_owner * rows + block_place[:, None]
    tof_row = block_owner[:, 0][None, :] * rows + block_place[None, :]
    tc = jnp.tile(tract_county.astype(F32), LANES // rows)[None, :]
    cs = jnp.concatenate(
        [
            county_answers * query_precision[2:3],
            state_answers * query_precision[3:4],
            jnp.zeros((-(counties + 1) % 16, queries), F32),
        ]
    )
    mt = jnp.pad(query_members.T, ((0, 0), (0, padded - cells)))
    vmem = pl.BlockSpec(memory_space=pltpu.VMEM)
    binary = (2,) * nb
    copies = 8 * nb
    shape = jax.ShapeDtypeStruct
    rbufs = [
        pltpu.VMEM((2,) * (nb - k - 1) + (rows, half), F32) for _ in range(2) for k in range(nb)
    ]
    outs = pl.pallas_call(
        functools.partial(tree_kernel, n),
        out_shape=[shape((tracts, queries), BF16)] * 4
        + [
            shape((queries, padded), BF16),
            shape((8, padded), F32),
            shape((2, groups, LANES), F32),
            shape((counties, padded), F32),
            shape((counties, padded), F32),
        ],
        in_specs=[vmem] * 8,
        out_specs=[vmem] * 9,
        scratch_shapes=[
            pltpu.VMEM(binary + (rows, queries), F32),
            pltpu.VMEM(binary + (rows, queries), F32),
            pltpu.VMEM(binary + (rows, queries), F32),
            pltpu.VMEM((2,) * (CHUNKS.bit_length() - 1) + (2, counties, LANES), F32),
            pltpu.VMEM((n, groups + 8, LANES), F32),
            pltpu.SemaphoreType.DMA((n,)),
            pltpu.SemaphoreType.DMA((n,)),
            pltpu.SemaphoreType.DMA((copies,)),
            pltpu.SemaphoreType.DMA((copies,)),
        ]
        + rbufs,
        compiler_params=pltpu.CompilerParams(
            collective_id=0, has_side_effects=True, vmem_limit_bytes=56 * 1024 * 1024
        ),
        name="tree",
    )(block_answers, tof_row, tof_col, tract_answers, tc, cs, mt, query_precision)

    own = (lax.axis_index("wide") * rows + jnp.arange(rows, dtype=jnp.int32))[:, None]
    tile = 256
    whole = lambda a: pl.BlockSpec(a.shape, lambda i: (0,) * a.ndim)
    return pl.pallas_call(
        histogram_kernel,
        grid=(blocks // tile,),
        out_shape=[
            shape((blocks, cells), F32),
            shape((rows, cells), F32),
            shape((counties, cells), F32),
        ],
        in_specs=[
            pl.BlockSpec((tile, queries), lambda i: (i, 0)),
            pl.BlockSpec((tile, 1), lambda i: (i, 0)),
            whole(own),
            whole(query_precision),
        ]
        + [whole(a) for a in outs],
        out_specs=[
            pl.BlockSpec((tile, cells), lambda i: (i, 0)),
            pl.BlockSpec((rows, cells), lambda i: (0, 0)),
            pl.BlockSpec((counties, cells), lambda i: (0, 0)),
        ],
        compiler_params=pltpu.CompilerParams(vmem_limit_bytes=56 * 1024 * 1024),
        name="histograms",
    )(block_answers, tof_col, own, query_precision, *outs)


def solution(mesh):
    in_specs = (
        P(("state", "wide"), None),
        P(("state", "wide"), None),
        P(("state", "wide")),
        P(("state", "wide"), None),
        P(("state", "wide")),
        P("state", None),
        P("state", None),
        P(),
        P(),
    )
    out_specs = (P(("state", "wide"), None), P(("state", "wide"), None), P("state", None))
    return jax.shard_map(local, mesh=mesh, in_specs=in_specs, out_specs=out_specs, check_vma=False)
```

profile of v0, /device:TPU:0, one launch (start us, length us, event | category | flops | bytes accessed | tf_op | source)
XLA Modules:
  0.0 133.6 jit_solution(4878170216683893928)
XLA Ops:
  0.6 0.7 convert_element_type.3
  1.3 0.7 broadcast_in_dim_tile.3.tc_ref
  2.0 0.1 pad.7.clone
  2.0 0.8 fusion
  2.8 0.6 iota_add_fusion.own_ref
  3.4 1.5 %pad.4.mt_ref = s32[8,2048]{1,0:T(8,128)} pad(s32[8,2016]{1,0:T(8,128)} %bitcast.4, s32[]{:T(128)} %constant.1.clone.1), padding=0_0x0_32 | pad | bytes 130052 | tf_op jit(solution)/shard_map/jit(_pad)/pad | solution.py:384
  4.9 0.9 broadcast_multiply_fusion
  5.8 0.8 maximum_maximum_fusion.cs_ref
  6.6 0.9 copy.14
  7.5 0.9 copy.15
  8.4 0.9 multiply_reduce_fusion
  9.3 1.3 add.26
  10.6 84.7 %tree.1 = (bf16[1024,512]{1,0:T(8,128)(2,1)}, bf16[1024,512]{1,0:T(8,128)(2,1)}, bf16[1024,512]{1,0:T(8,128)(2,1)}, bf16[1024,512]{1,0:T(8,128)(2,1)}, bf16[512,...) custom-call(f32[1024,512]{1,0:T(8,128)} %ba_ref.3, ...), custom_call_target="tpu_custom_call" | custom-call | tf_op jit(solution)/shard_map/tree/pallas_call | solution.py:392
  95.3 29.1 %histograms.1 = (f32[1024,2016]{1,0:T(8,128)}, f32[64,2016]{1,0:T(8,128)}, f32[88,2016]{1,0:T(8,128)}) custom-call(f32[1024,512]{1,0:T(8,128)} %ba_ref.3, s32[1024,1]{1,0:T(8,128)} %get-tuple-element.28.tof_col_ref.tof_ref, s32[64,1]{1,0:T(8,128)} %iota_add_fusion.own_ref, f32[4,512]{1,0:T(4,128)} %qp_ref.3, bf16[1024,512]{1,0:T(8,128)(2,1)} %get-tuple-element.12.g1h_ref, ...), custom_call_target="tpu_custom_call" | custom-call | tf_op jit(solution)/shard_map/histograms/pallas_call | solution.py:425
  124.4 9.2 %copy.16 = f32[1024,2016]{0,1:T(8,128)} copy(f32[1024,2016]{1,0:T(8,128)} %get-tuple-element.24) | data formatting | bytes 16515072 | tf_op jit(solution)/shard_map/histograms/pallas_call | solution.py:425
  (2 shorter events, 0.0 us)
where the time goes:
time: 134 us
  Pallas kernels  114 us (85%)
  local copies, waits for them, and re-layouts  13.2 us (10%)
  other arithmetic  5.9 us (4%)
    pallas_call x1, Pallas kernels, local(): pl.pallas_call(functools.partial(tree_kernel, n), out_shape=[shape((tract...  84.7 us
    pallas_call x1, Pallas kernels, local(): pl.pallas_call(histogram_kernel, grid=(blocks // tile,), out_shape=[shape...  29.1 us
    pallas_call x1, local copies, waits for them, and re-layouts, local(): pl.pallas_call(histogram_kernel, grid=(blocks // tile,), out_shape=[shape...  9.2 us

commit v1 on v0

v1 whole, which is shorter than its diff:
```python
import functools
import itertools

import jax
import jax.numpy as jnp
from jax import lax
from jax.experimental import pallas as pl
from jax.experimental.pallas import tpu as pltpu
from jax.sharding import PartitionSpec as P

LANES = 128
CHUNKS = 16
MESH = pl.DeviceIdType.MESH
F32 = jnp.float32
BF16 = jnp.bfloat16


def halves(x):
    high = x.astype(BF16)
    return high, (x - high.astype(F32)).astype(BF16)


def product(left, right):
    return jnp.dot(left, right, preferred_element_type=F32)


def two_products(high, low, right):
    return product(high, right) + product(low, right)


def picked(table, row_of):
    groups = table.shape[0]
    count = row_of.shape[0]
    wide = jnp.zeros((count, LANES), F32)
    for g in range(groups):
        wide = jnp.where(row_of // LANES == g, table[g : g + 1, :], wide)
    lane = lax.broadcasted_iota(jnp.int32, (count, LANES), 1)
    return jnp.sum(jnp.where(lane == row_of % LANES, wide, 0.0), axis=1, keepdims=True)


def nt_product(left, right):
    return lax.dot_general(left, right, (((1,), (1,)), ((), ())), preferred_element_type=F32)


def tree_kernel(
    n,
    ba_ref,
    owner_ref,
    place_ref,
    ta_ref,
    tc_ref,
    ca_ref,
    sa_ref,
    mt_ref,
    qp_ref,
    base_ref,
    cov_ref,
    covt_ref,
    nk_ref,
    own_ref,
    tbase_ref,
    rate_ref,
    hist_ref,
    acc,
    g1,
    gs,
    g2,
    misc,
    mpad,
    cover_ref,
    covert_ref,
    tofc,
    high_ref,
    low_ref,
    misc_send,
    misc_recv,
    send_sems,
    recv_sems,
    *rbufs,
):
    nb = n.bit_length() - 1
    me = lax.axis_index("wide")
    rows, queries = ta_ref.shape
    blocks = ba_ref.shape[0]
    cells = cover_ref.shape[1]
    groups = n * rows // LANES
    counties = rate_ref.shape[0]
    tile = 256
    tall = 512
    half = queries // 2
    bit = [(me // (1 << b)) % 2 for b in range(nb)]
    orders = [list(range(nb)), [0] + list(range(2, nb)) + [1]]
    cols = [pl.ds(0, half), pl.ds(half, half)]
    used = [0]
    sends = []

    def partner(b):
        return me + (1 - 2 * bit[b]) * (1 << b)

    def remote(src, dst, b):
        k = used[0]
        used[0] += 1
        copy = pltpu.make_async_remote_copy(
            src_ref=src,
            dst_ref=dst,
            send_sem=send_sems.at[k],
            recv_sem=recv_sems.at[k],
            device_id={"wide": partner(b)},
            device_id_type=MESH,
        )
        copy.start()
        sends.append(copy)
        return copy

    def at(values, low=0):
        return tuple(values[b] for b in range(nb - 1, low - 1, -1))

    def scatter_start(g, k):
        order = orders[g]
        values = [slice(None)] * nb
        for b in order[:k]:
            values[b] = bit[b]
        values[order[k]] = 1 - bit[order[k]]
        src = acc.at[at(values) + (slice(None), cols[g])]
        return remote(src, rbufs[g * nb + k], order[k])

    def scatter_add(g, k):
        order = orders[g]
        rest = sorted(order[k + 1 :], reverse=True)
        for combo in itertools.product((0, 1), repeat=len(rest)):
            values = list(bit)
            for b, v in zip(rest, combo):
                values[b] = v
            spot = at(values) + (slice(None), cols[g])
            acc[spot] = acc[spot] + rbufs[g * nb + k][combo + (slice(None), slice(None))]

    def gather_start(buf, order, k, tail, low=0):
        values = list(bit)
        for b in order[:k]:
            values[b] = slice(None)
        ref = buf.at[at(values, low) + tail]
        return remote(ref, ref, order[k])

    barrier = pltpu.get_barrier_semaphore()
    for k in range(1, n):
        pl.semaphore_signal(
            barrier, inc=1, device_id={"wide": lax.rem(me + k, n)}, device_id_type=MESH
        )
    pl.semaphore_wait(barrier, n - 1)

    back = [list(reversed(o)) for o in orders]
    g1[at(bit)] = ta_ref[...] * qp_ref[1:2, :]
    tract_copies = [gather_start(g1, back[g], 0, (slice(None), cols[g])) for g in range(2)]

    tof_row = owner_ref[...] * rows + place_ref[...]
    tofc[...] = jnp.broadcast_to(tof_row.astype(F32), (LANES, blocks)).T.astype(jnp.int32)
    tof_col = tofc[:, 0:1]
    row_hot = (lax.broadcasted_iota(jnp.int32, (groups, blocks), 0) == tof_row // LANES).astype(BF16)
    col_hot = (lax.broadcasted_iota(jnp.int32, (blocks, LANES), 1) == tof_col % LANES).astype(BF16)
    misc[me, :groups, :] = product(row_hot, col_hot)
    lane = lax.broadcasted_iota(jnp.int32, (8, LANES), 1)
    mine = lane // rows == me % (LANES // rows)
    misc[me, groups:, :] = jnp.where(mine, jnp.concatenate([tc_ref[...].astype(F32)] * (LANES // rows), axis=1), 0.0)
    misc_copies = []
    for k in range(1, n):
        copy = pltpu.make_async_remote_copy(
            src_ref=misc.at[me],
            dst_ref=misc.at[me],
            send_sem=misc_send.at[k],
            recv_sem=misc_recv.at[k],
            device_id={"wide": lax.rem(me + k, n)},
            device_id_type=MESH,
        )
        copy.start()
        misc_copies.append(copy)

    xh, xl = halves(ba_ref[...] * qp_ref[0:1, :])
    step = min(4, n)
    for c in range(n // step):
        label = lax.broadcasted_iota(jnp.int32, (step * rows, blocks), 0) + c * step * rows
        hot = (label == tof_row).astype(BF16)
        part = product(hot, xh) + product(hot, xl)
        for s in range(step):
            w = c * step + s
            spot = tuple((w >> b) & 1 for b in range(nb - 1, -1, -1))
            acc[spot] = part[s * rows : (s + 1) * rows]

    sums = [scatter_start(g, 0) for g in range(2)]

    mpad[...] = jnp.zeros_like(mpad)
    mpad[:, : mt_ref.shape[1]] = mt_ref[...]

    def cover_lanes(i, carry):
        spot = pl.ds(pl.multiple_of(i * LANES, LANES), LANES)
        label = lax.broadcasted_iota(jnp.int32, (queries, LANES), 0)
        total = jnp.zeros((queries, LANES), F32)
        for m in range(mpad.shape[0]):
            total = total + jnp.where(label == mpad[m : m + 1, spot], 1.0, 0.0)
        cover_ref[:, spot] = total.astype(BF16)
        covert_ref[spot, :] = total.T.astype(BF16)
        return carry

    lax.fori_loop(0, cells // LANES, cover_lanes, 0)
    weights = jnp.concatenate([qp_ref[...], qp_ref[...]], axis=0)
    w0, _ = halves(weights)
    w1, w2 = halves(weights - w0.astype(F32))
    cover = cover_ref[...]
    coverage = product(w0, cover) + product(w1, cover) + product(w2, cover)
    cov_ref[...] = coverage
    blank = jnp.zeros((LANES - 8, LANES), F32)
    for c in range(cells // LANES):
        piece = slice(c * LANES, (c + 1) * LANES)
        covt_ref[piece, :] = jnp.concatenate([coverage[:, piece], blank], axis=0).T

    def blocks_part(j):
        spot = slice(j * tile, (j + 1) * tile)
        xh, xl = halves(ba_ref[spot, :] * qp_ref[0:1, :])

        def body(i, carry):
            down = pl.ds(pl.multiple_of(i * tall, tall), tall)
            left = covert_ref[down, :]
            total = nt_product(left, xh) + nt_product(left, xl)
            base_ref[down, spot] = total * (1.0 / covt_ref[down, 0:1])
            return carry

        lax.fori_loop(0, cells // tall, body, 0)

    def tracts_part(j, of_sums):
        spot = slice(j * tile, (j + 1) * tile)
        label = lax.broadcasted_iota(jnp.int32, (tile, n * rows), 1)
        hot = (label == tofc[spot, 0:1]).astype(BF16)
        ph = product(hot, high_ref[...]).astype(BF16)
        pl_ = product(hot, low_ref[...]).astype(BF16)
        n_row = nk_ref[0:1, spot]

        def body(i, carry):
            down = pl.ds(pl.multiple_of(i * tall, tall), tall)
            left = covert_ref[down, :]
            total = nt_product(left, ph) + nt_product(left, pl_)
            c0, c1 = covt_ref[down, 0:1], covt_ref[down, 1:2]
            if of_sums:
                total = total * (-c1 / c0)
            base_ref[down, spot] = base_ref[down, spot] + total / (n_row * c1 + c0)
            return carry

        lax.fori_loop(0, cells // tall, body, 0)

    parts = blocks // tile
    for k in range(nb):
        if k:
            for j in range(parts):
                if j % (nb - 1) == k - 1:
                    blocks_part(j)
        for g in range(2):
            sums[g].wait_recv()
            scatter_add(g, k)
            if k + 1 < nb:
                sums[g] = scatter_start(g, k + 1)
        for g in range(2):
            tract_copies[g].wait_recv()
            if k + 1 < nb:
                tract_copies[g] = gather_start(g1, back[g], k + 1, (slice(None), cols[g]))
    gs[at(bit)] = acc[at(bit)]
    sums = [gather_start(gs, back[g], 0, (slice(None), cols[g])) for g in range(2)]

    for copy in misc_copies:
        copy.wait_recv()
    counts = misc[0, :groups, :]
    for d in range(1, n):
        counts = counts + misc[d, :groups, :]
    per = LANES // rows
    county_rows = []
    for j in range(groups):
        row = misc[j * per, groups : groups + 1, :]
        for i in range(1, per):
            row = row + misc[j * per + i, groups : groups + 1, :]
        county_rows.append(row)
    county_table = jnp.concatenate(county_rows, axis=0)
    n_col = picked(counts, lax.broadcasted_iota(jnp.int32, (n * rows, 1), 0))
    nk_ref[0:1, :] = jnp.broadcast_to(picked(counts, tofc[:, 0:1]), (blocks, LANES)).T[0:1]
    nk_ref[1:2, :] = jnp.broadcast_to(picked(county_table, tofc[:, 0:1]), (blocks, LANES)).T[0:1]
    mine_id = lax.broadcasted_iota(jnp.int32, (rows, 1), 0) + me * rows
    n_own = picked(counts, mine_id)
    own_ref[:, 0:1] = n_own
    own_ref[:, 1:2] = picked(county_table, mine_id)

    def spot_of(w):
        return tuple((w >> b) & 1 for b in range(nb - 1, -1, -1))

    def split_into(value_of):
        for w in range(n):
            high, low = halves(value_of(w))
            high_ref[w * rows : (w + 1) * rows, :] = high
            low_ref[w * rows : (w + 1) * rows, :] = low

    def stacked(x, right):
        high, low = halves(x)
        both = product(jnp.concatenate([high, low], axis=0), right)
        return both[: x.shape[0]] + both[x.shape[0] :]

    low_bit = nb - (CHUNKS.bit_length() - 1)
    chunk = me // (1 << low_bit)
    lanes = pl.ds(pl.multiple_of(chunk * LANES, LANES), LANES)
    cov = cover_ref[:, lanes]
    c0, c1, c2, c3 = [cov_ref[l : l + 1, lanes] for l in range(4)]
    v2, v3 = 1.0 / c2, 1.0 / c3
    county_measured = stacked(ca_ref[...] * qp_ref[2:3, :], cov) * v2
    state_row = jnp.broadcast_to(sa_ref[...] * qp_ref[3:4, :], (16, queries))
    state_measured = stacked(state_row, cov)[0:1] * v3
    split_into(lambda w: g1[spot_of(w)])

    for k in range(nb):
        for j in range(parts):
            if j % nb == k:
                tracts_part(j, False)
        if k == 0:
            own_sum = n_own * (ta_ref[...] * qp_ref[1:2, :]) + acc[at(bit)]
            tbase_ref[...] = stacked(own_sum, cover_ref[...])
        for g in range(2):
            sums[g].wait_recv()
            if k + 1 < nb:
                sums[g] = gather_start(gs, back[g], k + 1, (slice(None), cols[g]))
    split_into(lambda w: n_col[w * rows : (w + 1) * rows] * g1[spot_of(w)] + gs[spot_of(w)])
    total = two_products(high_ref[...], low_ref[...], cov)
    factor = 1.0 / (n_col * c1 + c0)
    joined = total * factor
    spread = n_col * factor
    jh, jl = halves(joined)
    sh, sl = halves(spread)
    both = jnp.concatenate([jh, jl, sh, sl], axis=1)
    sums4 = jnp.zeros((counties, 4 * LANES), F32)
    for j in range(groups):
        label = lax.broadcasted_iota(jnp.int32, (counties, LANES), 0).astype(F32)
        hot = (label == county_rows[j]).astype(BF16)
        sums4 += product(hot, both[j * LANES : (j + 1) * LANES])
    county_child = sums4[:, :LANES] + sums4[:, LANES : 2 * LANES]
    county_child_spread = sums4[:, 2 * LANES : 3 * LANES] + sums4[:, 3 * LANES :]
    county_total = county_child_spread + v2
    county_joined = (county_child_spread * county_measured + v2 * county_child) / county_total
    county_spread = county_child_spread * v2 / county_total
    state_sum = jnp.sum(county_joined, axis=0, keepdims=True)
    state_spread = jnp.sum(county_spread, axis=0, keepdims=True)
    state_rate = (state_measured - state_sum) / (state_spread + v3)
    spot = at(bit, low_bit)
    g2[spot + (0,)] = (county_measured - county_child + v2 * state_rate) / county_total
    g2[spot + (1,)] = county_joined + county_spread * state_rate
    short = [[b for b in o if b >= low_bit] for o in back]
    last = [gather_start(g2, short[g], 0, (g,), low_bit) for g in range(2)]
    split_into(lambda w: gs[spot_of(w)])
    for k in range(len(short[0])):
        for j in range(parts):
            if j % len(short[0]) == k:
                tracts_part(j, True)
        for g in range(2):
            last[g].wait_recv()
            if k + 1 < len(short[0]):
                last[g] = gather_start(g2, short[g], k + 1, (g,), low_bit)
    for c in range(CHUNKS):
        spot = tuple((c >> b) & 1 for b in range(CHUNKS.bit_length() - 2, -1, -1))
        rate_ref[:, c * LANES : (c + 1) * LANES] = g2[spot + (0,)]
        hist_ref[:, c * LANES : (c + 1) * LANES] = g2[spot + (1,)]
    for copy in sends + misc_copies:
        copy.wait_send()


def histogram_kernel(
    base_ref, cov_ref, covt_ref, nk_ref, own_ref, tbase_ref, rate_ref, hist_ref,
    block_ref, tract_ref, county_ref,
):
    counties, width = rate_ref.shape
    blocks = nk_ref.shape[1]
    rows = own_ref.shape[0]
    rate = jnp.concatenate([rate_ref[...], jnp.zeros((LANES - counties, width), F32)], axis=0)
    rh, rl = halves(rate.T)
    label = lax.broadcasted_iota(jnp.int32, (LANES, blocks), 0).astype(F32)
    hot = (label == nk_ref[1:2, :]).astype(BF16)
    above = two_products(rh, rl, hot)
    c0, c1 = covt_ref[:, 0:1], covt_ref[:, 1:2]
    block_ref[...] = base_ref[...] + above / (nk_ref[0:1, :] * c1 + c0)

    label = lax.broadcasted_iota(jnp.int32, (rows, LANES), 1).astype(F32)
    hot = (label == own_ref[:, 1:2]).astype(BF16)
    rh, rl = halves(rate)
    n_own = own_ref[:, 0:1]
    above = product(hot, rh) + product(hot, rl)
    tract_ref[...] = (tbase_ref[...] + n_own * above) / (n_own * cov_ref[1:2, :] + cov_ref[0:1, :])
    county_ref[...] = hist_ref[...]


def local(
    block_answers,
    block_owner,
    block_place,
    tract_answers,
    tract_county,
    county_answers,
    state_answers,
    query_members,
    query_precision,
):
    n = lax.axis_size("wide")
    nb = n.bit_length() - 1
    blocks, queries = block_answers.shape
    rows = tract_answers.shape[0]
    tracts = rows * n
    cells = query_members.shape[0]
    counties = county_answers.shape[0]
    padded = CHUNKS * LANES
    groups = tracts // LANES
    half = queries // 2
    vmem = pl.BlockSpec(memory_space=pltpu.VMEM)
    binary = (2,) * nb
    copies = 8 * nb
    shape = jax.ShapeDtypeStruct
    rbufs = [
        pltpu.VMEM((2,) * (nb - k - 1) + (rows, half), F32) for _ in range(2) for k in range(nb)
    ]
    outs = pl.pallas_call(
        functools.partial(tree_kernel, n),
        out_shape=[
            shape((padded, blocks), F32),
            shape((8, padded), F32),
            shape((padded, LANES), F32),
            shape((8, blocks), F32),
            shape((rows, LANES), F32),
            shape((rows, padded), F32),
            shape((counties, padded), F32),
            shape((counties, padded), F32),
        ],
        in_specs=[vmem] * 9,
        out_specs=[vmem] * 8,
        scratch_shapes=[
            pltpu.VMEM(binary + (rows, queries), F32),
            pltpu.VMEM(binary + (rows, queries), F32),
            pltpu.VMEM(binary + (rows, queries), F32),
            pltpu.VMEM((2,) * (CHUNKS.bit_length() - 1) + (2, counties, LANES), F32),
            pltpu.VMEM((n, groups + 8, LANES), F32),
            pltpu.VMEM((query_members.shape[1], padded), jnp.int32),
            pltpu.VMEM((queries, padded), BF16),
            pltpu.VMEM((padded, queries), BF16),
            pltpu.VMEM((blocks, LANES), jnp.int32),
            pltpu.VMEM((tracts, queries), BF16),
            pltpu.VMEM((tracts, queries), BF16),
            pltpu.SemaphoreType.DMA((n,)),
            pltpu.SemaphoreType.DMA((n,)),
            pltpu.SemaphoreType.DMA((copies,)),
            pltpu.SemaphoreType.DMA((copies,)),
        ]
        + rbufs,
        compiler_params=pltpu.CompilerParams(
            collective_id=0, has_side_effects=True, vmem_limit_bytes=56 * 1024 * 1024
        ),
        name="tree",
    )(
        block_answers,
        block_owner.T,
        block_place[None, :],
        tract_answers,
        tract_county[None, :],
        county_answers,
        state_answers,
        query_members.T,
        query_precision,
    )

    tile = 256
    down = lambda a: pl.BlockSpec((tile, a.shape[1]), lambda i: (i, 0))
    across = lambda a: pl.BlockSpec((a.shape[0], tile), lambda i: (0, i))
    whole = lambda a: pl.BlockSpec(a.shape, lambda i: (0, 0))
    kinds = [down, across, down, whole, whole, across, across, across]
    block_histogram, tract_histogram, county_histogram = pl.pallas_call(
        histogram_kernel,
        grid=(padded // tile,),
        out_shape=[
            shape((cells, blocks), F32),
            shape((rows, cells), F32),
            shape((counties, cells), F32),
        ],
        in_specs=[kind(a) for kind, a in zip(kinds, outs)],
        out_specs=[
            pl.BlockSpec((tile, blocks), lambda i: (i, 0)),
            pl.BlockSpec((rows, tile), lambda i: (0, i)),
            pl.BlockSpec((counties, tile), lambda i: (0, i)),
        ],
        compiler_params=pltpu.CompilerParams(vmem_limit_bytes=56 * 1024 * 1024),
        name="histograms",
    )(*outs)
    return block_histogram.T, tract_histogram, county_histogram


def solution(mesh):
    in_specs = (
        P(("state", "wide"), None),
        P(("state", "wide"), None),
        P(("state", "wide")),
        P(("state", "wide"), None),
        P(("state", "wide")),
        P("state", None),
        P("state", None),
        P(),
        P(),
    )
    out_specs = (P(("state", "wide"), None), P(("state", "wide"), None), P("state", None))
    return jax.shard_map(local, mesh=mesh, in_specs=in_specs, out_specs=out_specs, check_vma=False)
```

time: 134 us -> 105 us (0.78)
  local copies, waits for them, and re-layouts: 13.2 us -> 0 us
  Pallas kernels: 114 us -> 104 us
  other arithmetic: 5.9 us -> 0 us
    pallas_call x2, Pallas kernels: 114 us -> 104 us  [the longest x1 92.7 us: local(): pl.pallas_call(functools.partial(tree_kernel, n), out_shape=[shape((padde...]
    pallas_call x1 -> x0, local copies, waits for them, and re-layouts: 9.2 us -> none  [local(): pl.pallas_call(histogram_kernel, grid=(blocks // tile,), out_shape=[shape...]
    add x2 -> x0, other arithmetic: 1.88 us -> none  [the longest x1 1.28 us: local(): tof_row = block_owner[:, 0][None, :] * rows + block_place[None, :]]
    mul x2 -> x0, other arithmetic: 1.81 us -> none  [the longest x1 0.94 us: local(): county_answers * query_precision[2:3]]
    pad x1 -> x0, local copies, waits for them, and re-layouts: 1.47 us -> none  [local(): mt = jnp.pad(query_members.T, ((0, 0), (0, padded - cells)))]
where the time goes in v1:
time: 105 us
  Pallas kernels  104 us (99%)
    pallas_call x1, Pallas kernels, local(): pl.pallas_call(functools.partial(tree_kernel, n), out_shape=[shape((padde...  92.7 us
    pallas_call x1, Pallas kernels, local(): pl.pallas_call(histogram_kernel, grid=(padded // tile,), out_shape=[shape...  11.6 us

profile of v1, /device:TPU:0, one launch (start us, length us, event | category | flops | bytes accessed | tf_op | source)
XLA Modules:
  0.0 105.1 jit_solution(14333116125899898482)
XLA Ops:
  0.6 92.7 %tree.1 = (f32[2048,1024]{1,0:T(8,128)}, f32[8,2048]{1,0:T(8,128)}, f32[2048,128]{1,0:T(8,128)}, f32[8,1024]{1,0:T(8,128)}, f32[64,128]{1,0:T(8,128)}, /*index=5...) custom-call(f32[1024,512]{1,0:T(8,128)} %ba_ref.1, s32[1,1024]{1,0:T(1,128)} %bitcast.6, s32[1,1024]{1,0:T(1,128)} %bitcast.7, ...), custom_call_target="tpu_custom_call" | custom-call | tf_op jit(solution)/shard_map/tree/pallas_call | solution.py:418
  93.3 11.6 %histograms.1 = (f32[2016,1024]{1,0:T(8,128)}, f32[64,2016]{1,0:T(8,128)}, f32[88,2016]{1,0:T(8,128)}) custom-call(f32[2048,1024]{1,0:T(8,128)} %get-tuple-element.14.base_ref, f32[8,2048]{1,0:T(8,128)} %get-tuple-element.15.cov_ref, f32[2048,128]{1,0:T(8,128)} %get-tuple-element.16.covt_ref, f32[8,1024]{1,0:T(8,128)} %get-tuple-element.17.nk_ref, ...), custom_call_target="tpu_custom_call" | custom-call | tf_op jit(solution)/shard_map/histograms/pallas_call | solution.py:471

commit v2 on v1

--- a/solution.py
+++ b/solution.py
@@ -185,6 +185,13 @@
             spot = tuple((w >> b) & 1 for b in range(nb - 1, -1, -1))
             acc[spot] = part[s * rows : (s + 1) * rows]
 
+    def tract_step(k):
+        for g in range(2):
+            tract_copies[g].wait_recv()
+            if k + 1 < nb:
+                tract_copies[g] = gather_start(g1, back[g], k + 1, (slice(None), cols[g]))
+
+    tract_step(0)
     sums = [scatter_start(g, 0) for g in range(2)]
 
     mpad[...] = jnp.zeros_like(mpad)
@@ -212,19 +219,6 @@
         piece = slice(c * LANES, (c + 1) * LANES)
         covt_ref[piece, :] = jnp.concatenate([coverage[:, piece], blank], axis=0).T
 
-    def blocks_part(j):
-        spot = slice(j * tile, (j + 1) * tile)
-        xh, xl = halves(ba_ref[spot, :] * qp_ref[0:1, :])
-
-        def body(i, carry):
-            down = pl.ds(pl.multiple_of(i * tall, tall), tall)
-            left = covert_ref[down, :]
-            total = nt_product(left, xh) + nt_product(left, xl)
-            base_ref[down, spot] = total * (1.0 / covt_ref[down, 0:1])
-            return carry
-
-        lax.fori_loop(0, cells // tall, body, 0)
-
     def tracts_part(j, of_sums):
         spot = slice(j * tile, (j + 1) * tile)
         label = lax.broadcasted_iota(jnp.int32, (tile, n * rows), 1)
@@ -232,6 +226,9 @@
         ph = product(hot, high_ref[...]).astype(BF16)
         pl_ = product(hot, low_ref[...]).astype(BF16)
         n_row = nk_ref[0:1, spot]
+        if not of_sums:
+            near = ph.astype(F32) + pl_.astype(F32) + ba_ref[spot, :] * qp_ref[0:1, :]
+            ph, pl_ = halves(near)
 
         def body(i, carry):
             down = pl.ds(pl.multiple_of(i * tall, tall), tall)
@@ -239,35 +236,36 @@
             total = nt_product(left, ph) + nt_product(left, pl_)
             c0, c1 = covt_ref[down, 0:1], covt_ref[down, 1:2]
             if of_sums:
-                total = total * (-c1 / c0)
-            base_ref[down, spot] = base_ref[down, spot] + total / (n_row * c1 + c0)
+                scaled = total * (c1 / c0) / (n_row * c1 + c0)
+                base_ref[down, spot] = base_ref[down, spot] - scaled
+            else:
+                base_ref[down, spot] = total * (1.0 / c0)
             return carry
 
         lax.fori_loop(0, cells // tall, body, 0)
 
     parts = blocks // tile
     for k in range(nb):
-        if k:
-            for j in range(parts):
-                if j % (nb - 1) == k - 1:
-                    blocks_part(j)
         for g in range(2):
             sums[g].wait_recv()
             scatter_add(g, k)
             if k + 1 < nb:
                 sums[g] = scatter_start(g, k + 1)
-        for g in range(2):
-            tract_copies[g].wait_recv()
-            if k + 1 < nb:
-                tract_copies[g] = gather_start(g1, back[g], k + 1, (slice(None), cols[g]))
-    gs[at(bit)] = acc[at(bit)]
-    sums = [gather_start(gs, back[g], 0, (slice(None), cols[g])) for g in range(2)]
+        if k != 1 and k < nb - 1:
+            tract_step(1 if k == 0 else k)
 
     for copy in misc_copies:
         copy.wait_recv()
     counts = misc[0, :groups, :]
     for d in range(1, n):
         counts = counts + misc[d, :groups, :]
+    mine_id = lax.broadcasted_iota(jnp.int32, (rows, 1), 0) + me * rows
+    n_own = picked(counts, mine_id)
+    own_sum = n_own * (ta_ref[...] * qp_ref[1:2, :]) + acc[at(bit)]
+    gs[at(bit)] = own_sum
+    sums = [gather_start(gs, back[g], 0, (slice(None), cols[g])) for g in range(2)]
+    tract_step(nb - 1)
+
     per = LANES // rows
     county_rows = []
     for j in range(groups):
@@ -279,8 +277,6 @@
     n_col = picked(counts, lax.broadcasted_iota(jnp.int32, (n * rows, 1), 0))
     nk_ref[0:1, :] = jnp.broadcast_to(picked(counts, tofc[:, 0:1]), (blocks, LANES)).T[0:1]
     nk_ref[1:2, :] = jnp.broadcast_to(picked(county_table, tofc[:, 0:1]), (blocks, LANES)).T[0:1]
-    mine_id = lax.broadcasted_iota(jnp.int32, (rows, 1), 0) + me * rows
-    n_own = picked(counts, mine_id)
     own_ref[:, 0:1] = n_own
     own_ref[:, 1:2] = picked(county_table, mine_id)
 
@@ -314,13 +310,12 @@
             if j % nb == k:
                 tracts_part(j, False)
         if k == 0:
-            own_sum = n_own * (ta_ref[...] * qp_ref[1:2, :]) + acc[at(bit)]
             tbase_ref[...] = stacked(own_sum, cover_ref[...])
         for g in range(2):
             sums[g].wait_recv()
             if k + 1 < nb:
                 sums[g] = gather_start(gs, back[g], k + 1, (slice(None), cols[g]))
-    split_into(lambda w: n_col[w * rows : (w + 1) * rows] * g1[spot_of(w)] + gs[spot_of(w)])
+    split_into(lambda w: gs[spot_of(w)])
     total = two_products(high_ref[...], low_ref[...], cov)
     factor = 1.0 / (n_col * c1 + c0)
     joined = total * factor
@@ -346,7 +341,6 @@
     g2[spot + (1,)] = county_joined + county_spread * state_rate
     short = [[b for b in o if b >= low_bit] for o in back]
     last = [gather_start(g2, short[g], 0, (g,), low_bit) for g in range(2)]
-    split_into(lambda w: gs[spot_of(w)])
     for k in range(len(short[0])):
         for j in range(parts):
             if j % len(short[0]) == k:

time: 105 us -> 99.7 us (0.950)
  Pallas kernels: 104 us -> 98.5 us
    pallas_call x1, Pallas kernels: 92.7 us -> 86.9 us  [local(): pl.pallas_call(functools.partial(tree_kernel, n), out_shape=[shape((padde...]
where the time goes in v2:
time: 99.7 us; the launch traced here: 99.3 us
  Pallas kernels  98.5 us (99%)
    pallas_call x1, Pallas kernels, local(): pl.pallas_call(functools.partial(tree_kernel, n), out_shape=[shape((padde...  86.9 us
    pallas_call x1, Pallas kernels, local(): pl.pallas_call(histogram_kernel, grid=(padded // tile,), out_shape=[shape...  11.6 us

profile of v2, /device:TPU:0, one launch (start us, length us, event | category | flops | bytes accessed | tf_op | source)
XLA Modules:
  0.0 99.3 jit_solution(14369321342342283558)
XLA Ops:
  0.6 86.9 %tree.1 = (f32[2048,1024]{1,0:T(8,128)}, f32[8,2048]{1,0:T(8,128)}, f32[2048,128]{1,0:T(8,128)}, f32[8,1024]{1,0:T(8,128)}, f32[64,128]{1,0:T(8,128)}, /*index=5...) custom-call(f32[1024,512]{1,0:T(8,128)} %ba_ref.1, s32[1,1024]{1,0:T(1,128)} %bitcast.6, s32[1,1024]{1,0:T(1,128)} %bitcast.7, ...), custom_call_target="tpu_custom_call" | custom-call | tf_op jit(solution)/shard_map/tree/pallas_call | solution.py:412
  87.6 11.6 %histograms.1 = (f32[2016,1024]{1,0:T(8,128)}, f32[64,2016]{1,0:T(8,128)}, f32[88,2016]{1,0:T(8,128)}) custom-call(f32[2048,1024]{1,0:T(8,128)} %get-tuple-element.14.base_ref, f32[8,2048]{1,0:T(8,128)} %get-tuple-element.15.cov_ref, f32[2048,128]{1,0:T(8,128)} %get-tuple-element.16.covt_ref, f32[8,1024]{1,0:T(8,128)} %get-tuple-element.17.nk_ref, ...), custom_call_target="tpu_custom_call" | custom-call | tf_op jit(solution)/shard_map/histograms/pallas_call | solution.py:465

commit v3 on v2

--- a/solution.py
+++ b/solution.py
@@ -194,6 +194,16 @@
     tract_step(0)
     sums = [scatter_start(g, 0) for g in range(2)]
 
+    def scatter_step(k):
+        for g in range(2):
+            sums[g].wait_recv()
+            scatter_add(g, k)
+            if k + 1 < nb:
+                sums[g] = scatter_start(g, k + 1)
+
+    scatter_step(0)
+    tract_step(1)
+
     mpad[...] = jnp.zeros_like(mpad)
     mpad[:, : mt_ref.shape[1]] = mt_ref[...]
 
@@ -245,15 +255,6 @@
         lax.fori_loop(0, cells // tall, body, 0)
 
     parts = blocks // tile
-    for k in range(nb):
-        for g in range(2):
-            sums[g].wait_recv()
-            scatter_add(g, k)
-            if k + 1 < nb:
-                sums[g] = scatter_start(g, k + 1)
-        if k != 1 and k < nb - 1:
-            tract_step(1 if k == 0 else k)
-
     for copy in misc_copies:
         copy.wait_recv()
     counts = misc[0, :groups, :]
@@ -261,6 +262,11 @@
         counts = counts + misc[d, :groups, :]
     mine_id = lax.broadcasted_iota(jnp.int32, (rows, 1), 0) + me * rows
     n_own = picked(counts, mine_id)
+    for k in range(1, nb):
+        scatter_step(k)
+        if 1 < k < nb - 1:
+            tract_step(k)
+
     own_sum = n_own * (ta_ref[...] * qp_ref[1:2, :]) + acc[at(bit)]
     gs[at(bit)] = own_sum
     sums = [gather_start(gs, back[g], 0, (slice(None), cols[g])) for g in range(2)]

time: 99.7 us -> 100 us (level)
  no operation moved by 1% of the time
where the time goes in v3:
time: 100 us; the launch traced here: 99.8 us
  Pallas kernels  99 us (99%)
    pallas_call x1, Pallas kernels, local(): pl.pallas_call(functools.partial(tree_kernel, n), out_shape=[shape((padde...  87.4 us
    pallas_call x1, Pallas kernels, local(): pl.pallas_call(histogram_kernel, grid=(padded // tile,), out_shape=[shape...  11.6 us

profile of v3, /device:TPU:0, one launch (start us, length us, event | category | flops | bytes accessed | tf_op | source)
XLA Modules:
  0.0 99.8 jit_solution(823678367946257236)
XLA Ops:
  0.6 87.4 %tree.1 = (f32[2048,1024]{1,0:T(8,128)}, f32[8,2048]{1,0:T(8,128)}, f32[2048,128]{1,0:T(8,128)}, f32[8,1024]{1,0:T(8,128)}, f32[64,128]{1,0:T(8,128)}, /*index=5...) custom-call(f32[1024,512]{1,0:T(8,128)} %ba_ref.1, s32[1,1024]{1,0:T(1,128)} %bitcast.6, s32[1,1024]{1,0:T(1,128)} %bitcast.7, ...), custom_call_target="tpu_custom_call" | custom-call | tf_op jit(solution)/shard_map/tree/pallas_call | solution.py:418
  88.1 11.6 %histograms.1 = (f32[2016,1024]{1,0:T(8,128)}, f32[64,2016]{1,0:T(8,128)}, f32[88,2016]{1,0:T(8,128)}) custom-call(f32[2048,1024]{1,0:T(8,128)} %get-tuple-element.14.base_ref, f32[8,2048]{1,0:T(8,128)} %get-tuple-element.15.cov_ref, f32[2048,128]{1,0:T(8,128)} %get-tuple-element.16.covt_ref, f32[8,1024]{1,0:T(8,128)} %get-tuple-element.17.nk_ref, ...), custom_call_target="tpu_custom_call" | custom-call | tf_op jit(solution)/shard_map/histograms/pallas_call | solution.py:471
